TPU v7x, 32 devices: a whole 2x2x4 slice. The times are simulated.
32 devices in a mesh: groups: 2 (over x), ctx: 8 (over z, y), head: 2 (over core).
Axes of the slice: x: 2, y: 2, z: 4, core: 2. Of those that a mesh axis runs over, the one named last changes fastest.
Arguments:
- queries: bfloat16 [256, 4096], P(('groups', 'ctx'), 'head'), parts along dimension 0, may hold values from -150 to 150
- cache_keys: bfloat16 [32768, 2048], P(('groups', 'ctx'), 'head'), parts along dimension 0, may hold values from -5 to 5
- cache_values: bfloat16 [32768, 2048], P(('groups', 'ctx'), 'head'), parts along dimension 0, may hold values from -6 to 6
- out_weight: bfloat16 [4096, 5376], P('head', 'ctx'), may hold values from -0.1875 to 0.1875
- norm_gain: float32 [5376], P('ctx'), may hold values from 0.1 to 1.9
Outputs:
- layer_output: bfloat16 [256, 5376], P(('groups', 'head'), 'ctx'), parts along dimension 0
There are 2 independent parts, one for each index of `groups`. A program takes and returns all parts, laid end to end along the dimension named above; an argument that names none is the same for every part. Nothing has to cross between parts.
All inputs are finite; a program needn't handle non-finite values.
Results may differ from a plain program's by a relative error of at most 0.0064.
Values may be sent and summed in bfloat16 or wider, within the bound.
A program may use at most 64 MiB of HBM per device.

v0:
```python
import jax
import jax.numpy as jnp
from jax import lax
from jax.sharding import PartitionSpec as P

D = 5376
HEADS = 32
KV_HEADS = 16
HEAD_DIM = 128


EPSILON = 1e-06


def attend(query_block, key_shard, value_shard):
    row_count = query_block.shape[0]
    group_size = HEADS // KV_HEADS
    head_width = group_size * HEAD_DIM
    softmax_scale = (D // HEADS) ** (-0.5)
    pair_count = key_shard.shape[1] // HEAD_DIM

    def one_head(head_index):
        query_part = lax.dynamic_slice_in_dim(query_block, head_index * head_width, head_width, 1)
        query_part = query_part.reshape(row_count, group_size, HEAD_DIM)
        key_part = lax.dynamic_slice_in_dim(key_shard, head_index * HEAD_DIM, HEAD_DIM, 1)
        value_part = lax.dynamic_slice_in_dim(value_shard, head_index * HEAD_DIM, HEAD_DIM, 1)
        scores = (
            jnp.einsum("rgd,kd->grk", query_part, key_part, preferred_element_type=jnp.float32)
            * softmax_scale
        )
        maxima = jnp.max(scores, axis=-1)
        expo = jnp.exp(scores - maxima[..., None])
        totals = jnp.sum(expo, axis=-1)
        probabilities = expo.astype(jnp.bfloat16)
        weighted = jnp.einsum(
            "grk,kd->rgd", probabilities, value_part, preferred_element_type=jnp.float32
        )
        weighted = weighted / totals.T[:, :, None]
        return (
            weighted.astype(jnp.bfloat16).reshape(row_count, head_width),
            (maxima + jnp.log(totals)).T,
        )

    outputs, log_totals = lax.map(one_head, jnp.arange(pair_count, dtype=jnp.int32))
    outputs = jnp.transpose(outputs, (1, 0, 2)).reshape(row_count, -1)
    log_totals = jnp.transpose(log_totals, (1, 0, 2)).reshape(row_count, -1)
    return (outputs, log_totals)


def local(queries, cache_keys, cache_values, out_weight, norm_gain):
    ctx_count = lax.axis_size("ctx")
    own_rows = queries.shape[0]
    local_width = queries.shape[1]
    local_heads = local_width // HEAD_DIM
    all_queries = lax.all_gather(queries, "ctx", axis=0, tiled=True)
    partials, log_totals = attend(all_queries, cache_keys, cache_values)
    grouped_out = partials.reshape(ctx_count, own_rows, local_width)
    grouped_lse = log_totals.reshape(ctx_count, own_rows, local_heads)
    arrived_out, arrived_lse = (
        lax.all_to_all(
            grouped_out.astype(jnp.float32), "ctx", split_axis=0, concat_axis=0, tiled=True
        ).astype(grouped_out.dtype),
        lax.all_to_all(grouped_lse, "ctx", split_axis=0, concat_axis=0, tiled=True),
    )
    peak_lse = jnp.max(arrived_lse, axis=0)
    whole_lse = peak_lse + jnp.log(jnp.sum(jnp.exp(arrived_lse - peak_lse[None]), axis=0))
    shard_weights = jnp.exp(arrived_lse - whole_lse[None])
    arrived_view = arrived_out.reshape(ctx_count, own_rows, local_heads, HEAD_DIM).astype(
        jnp.float32
    )
    attention = jnp.sum(arrived_view * shard_weights[..., None], axis=0).reshape(
        own_rows, local_width
    )
    attention = attention.astype(jnp.bfloat16)
    projected = jnp.dot(
        lax.all_gather(attention, "ctx", axis=0, tiled=True),
        out_weight,
        preferred_element_type=jnp.float32,
    )
    summed = lax.psum_scatter(projected, "head", scatter_dimension=0, tiled=True)
    square_sums = lax.psum(jnp.sum(summed * summed, axis=1), "ctx")
    inverse_rms = lax.rsqrt(square_sums / D + EPSILON)
    normed = summed * inverse_rms[:, None] * norm_gain[None, :]
    return normed.astype(jnp.bfloat16)


def solution(mesh):
    in_specs = (
        P(("groups", "ctx"), "head"),
        P(("groups", "ctx"), "head"),
        P(("groups", "ctx"), "head"),
        P("head", "ctx"),
        P("ctx"),
    )
    out_specs = P(("groups", "head"), "ctx")
    return jax.shard_map(local, mesh=mesh, in_specs=in_specs, out_specs=out_specs, check_vma=False)
```

profile of v0, /device:TPU:0, one launch (start us, length us, event | category | flops | bytes accessed | tf_op | source)
XLA Modules:
  0.0 190.1 jit_solution(6056905237629922939)
XLA Ops:
  6.5 33.3 %all_gather.6 = bf16[128,2048]{1,0:T(8,128)(2,1)S(1)} all-gather(bf16[16,2048]{1,0:T(8,128)(2,1)} %param.7), channel_id=1, replica_groups=mesh['groups'=2,'ctx'=8,'head'=2] {'ctx'}, dimensions={0}, use_global_device_ids=true | all-gather | bytes 589824 | tf_op jit(solution)/shard_map/all_gather | solution.py:55
  39.9 50.2 %while.12 = (s32[]{:T(128)}, bf16[8,128,256]{1,2,0:T(8,128)(2,1)}, f32[8,128,2]{1,2,0:T(2,128)S(1)}, s32[8]{0:T(128)S(1)}, bf16[2048,1024]{1,0:T(8,128)(2,1)}, /...) while((s32[]{:T(128)}, bf16[8,128,256]{1,2,0:T(8,128)(2,1)}, ...), condition=%wide.region_3.4_spmd, body=%wide.region_0.3_spmd.sunk | while | flops 271646464 | bytes 7873269 | solution.py:44
  39.9 0.7 dynamic_slice.31
  42.1 1.5 fusion.27
  44.0 1.6 fusion.29
  45.5 0.6 constant_dynamic-update-slice_fusion.4
  46.2 0.7 dynamic_slice.31
  48.4 1.5 fusion.27
  50.2 1.6 fusion.29
  52.4 0.7 dynamic_slice.31
  54.6 1.5 fusion.27
  56.5 1.6 fusion.29
  58.1 0.6 constant_dynamic-update-slice_fusion.4
  58.7 0.7 dynamic_slice.31
  60.9 1.5 fusion.27
  62.8 1.6 fusion.29
  64.3 0.6 constant_dynamic-update-slice_fusion.4
  65.0 0.7 dynamic_slice.31
  67.2 1.5 fusion.27
  69.0 1.6 fusion.29
  71.2 0.7 dynamic_slice.31
  73.4 1.5 fusion.27
  75.3 1.6 fusion.29
  76.9 0.6 constant_dynamic-update-slice_fusion.4
  77.5 0.7 dynamic_slice.31
  79.7 1.5 fusion.27
  81.6 1.6 fusion.29
  83.1 0.6 constant_dynamic-update-slice_fusion.4
  83.8 0.7 dynamic_slice.31
  86.0 1.5 fusion.27
  87.8 1.6 fusion.29
  90.2 0.7 reshape.31
  90.8 5.7 %all-to-all-start.1 = ((f32[8,1,256]{2,1,0:T(1,128)}), f32[8,1,256]{2,1,0:T(1,128)S(1)}, u32[]{:S(2)}, u32[]{:S(2)}) async-start(f32[8,1,256]{2,1,0:T(1,128)} %reshape.31), calls=%async_computation.1 | async-start | bytes 16384 | tf_op jit(solution)/shard_map/all_to_all | solution.py:63
  96.5 1.4 copy.24
  98.0 1.0 reshape.28
  99.0 4.1 %all-to-all-done.1 = f32[8,1,256]{2,1,0:T(1,128)S(1)} async-done(((f32[8,1,256]{2,1,0:T(1,128)}), f32[8,1,256]{2,1,0:T(1,128)S(1)}, u32[]{:S(2)}, u32[]{:S(2)}) %all-to-all-start.1) | async-done | bytes 8224 | tf_op jit(solution)/shard_map/all_to_all | solution.py:63
  103.2 3.5 %all-to-all-start = ((bf16[8,16,2048]{2,1,0:T(8,128)(2,1)}), bf16[8,16,2048]{2,1,0:T(8,128)(2,1)S(1)}, u32[]{:S(2)}, u32[]{:S(2)}) async-start(bf16[8,16,2048]{2,1,0:T(8,128)(2,1)} %reshape.28), calls=%async_computation | async-start | bytes 1048576 | tf_op jit(solution)/shard_map/all_to_all | solution.py:60
  107.2 0.7 reduce.1
  108.1 1.4 mul.49
  109.5 2.4 %mul.50 = f32[8,16,2048]{2,1,0:T(8,128)} reshape(f32[8,16,16,128]{3,2,1,0:T(8,128)} %mul.49) | data formatting | bytes 2097152 | tf_op jit(solution)/shard_map/mul | solution.py:71
  111.9 5.6 %all-to-all-done = bf16[8,16,2048]{2,1,0:T(8,128)(2,1)S(1)} async-done(((bf16[8,16,2048]{2,1,0:T(8,128)(2,1)}), bf16[8,16,2048]{2,1,0:T(8,128)(2,1)S(1)}, u32[]{:S(2)}, u32[]{:S(2)}) %all-to-all-start) | async-done | bytes 524320 | tf_op jit(solution)/shard_map/all_to_all | solution.py:60
  117.5 1.3 multiply_reduce_fusion
  118.9 31.2 %all_gather.7 = bf16[128,2048]{1,0:T(8,128)(2,1)S(1)} all-gather(bf16[16,2048]{1,0:T(8,128)(2,1)S(1)} %multiply_reduce_fusion), channel_id=1, replica_groups=mesh['groups'=2,'ctx'=8,'head'=2] {'ctx'}, dimensions={0}, use_global_device_ids=true | all-gather | bytes 589824 | tf_op jit(solution)/shard_map/all_gather | solution.py:76
  150.1 1.7 fusion.14
  151.9 7.1 %reduce-scatter.2.cloned.1.call-done = f32[64,672]{1,0:T(8,128)} async-done(((f32[128,672]{1,0:T(8,128)}), f32[64,672]{1,0:T(8,128)}) %reduce-scatter.2.cloned.1.call-update) | async-done | bytes 172048 | tf_op jit(solution)/shard_map/reduce_scatter | solution.py:80
  159.0 1.0 multiply_reduce_fusion.1
  160.0 21.6 %psum.7 = f32[64]{0:T(128)S(1)} all-reduce(f32[64]{0:T(128)S(1)} %multiply_reduce_fusion.1), channel_id=1, replica_groups=mesh['groups'=2,'ctx'=8,'head'=2] {'ctx'}, use_global_device_ids=true, to_apply=%region_9.10 | all-reduce | flops 64 | bytes 512 | tf_op jit(solution)/shard_map/psum | solution.py:81
  181.6 1.7 multiply_convert_fusion
  (54 shorter events, 6.3 us)
Async XLA Ops:
  6.5 143.6 %copy-start = (bf16[2048,672]{0,1:T(8,128)(2,1)S(1)}, bf16[2048,672]{0,1:T(8,128)(2,1)}, u32[]{:S(2)}) copy-start(bf16[2048,672]{0,1:T(8,128)(2,1)} %param.10) | copy-start | bytes 8257540
  90.8 12.3 %all-to-all-start.1 = ((f32[8,1,256]{2,1,0:T(1,128)}), f32[8,1,256]{2,1,0:T(1,128)S(1)}, u32[]{:S(2)}, u32[]{:S(2)}) async-start(f32[8,1,256]{2,1,0:T(1,128)} %reshape.31), calls=%async_computation.1 | async-start | bytes 16384 | tf_op jit(solution)/shard_map/all_to_all | solution.py:63
  103.2 14.4 %all-to-all-start = ((bf16[8,16,2048]{2,1,0:T(8,128)(2,1)}), bf16[8,16,2048]{2,1,0:T(8,128)(2,1)S(1)}, u32[]{:S(2)}, u32[]{:S(2)}) async-start(bf16[8,16,2048]{2,1,0:T(8,128)(2,1)} %reshape.28), calls=%async_computation | async-start | bytes 1048576 | tf_op jit(solution)/shard_map/all_to_all | solution.py:60
  106.7 52.3 %reduce-scatter.2.cloned.1.call-start = ((), (), s32[]{:S(2)}) async-start(), calls=%async_computation.3 | async-start | bytes 589824 | tf_op jit(solution)/shard_map/reduce_scatter | solution.py:80
  150.1 31.5 %copy-start.1 = (f32[672]{0:T(1024)S(1)}, f32[672]{0:T(1024)}, u32[]{:S(2)}) copy-start(f32[672]{0:T(1024)} %param.11) | copy-start | bytes 8068
Sparse Core Ops, SparseCore 0:
  152.0 6.9 reduce-scatter.1
where the time goes:
time: 192 us; the launch traced here: 190 us
  blocking collectives  86.2 us (45%)
  matrix products  26.5 us (14%)
  local copies, waits for them, and re-layouts  19.1 us (10%)
  waiting for transfers between devices  16.9 us (9%)
  between operations  13.5 us (7%)
  loops' own time  11.5 us (6%)
  starting transfers between devices  9.23 us (5%)
  other arithmetic  7.27 us (4%)
    all_gather x1, blocking collectives, local(): all_queries = lax.all_gather(queries, 'ctx', axis=0, tiled=True)  33.3 us
    all_gather x1, blocking collectives, local(): lax.all_gather(attention, 'ctx', axis=0, tiled=True)  31.2 us
    psum x1, blocking collectives, local(): square_sums = lax.psum(jnp.sum(summed * summed, axis=1), 'ctx')  21.6 us
    dot_general x8, matrix products, one_head(): jnp.einsum('grk,kd->rgd', probabilities, value_part, preferred_element_ty...  12.5 us
    dot_general x8, matrix products, one_head(): jnp.einsum('rgd,kd->grk', query_part, key_part, preferred_element_type=jn...  12.3 us
    another operation x1, loops' own time, attend(): lax.map(one_head, jnp.arange(pair_count, dtype=jnp.int32))  11.5 us
    reduce_scatter x1, waiting for transfers between devices, local(): lax.psum_scatter(projected, 'head', scatter_dimension=0, tiled=True)  7.12 us
    all_to_all x1, starting transfers between devices, local(): lax.all_to_all(grouped_lse, 'ctx', split_axis=0, concat_axis=0, tiled=True)  5.7 us
  transfers between devices with their start and end apart: 3, of which 3 were waited for; matrix products, arithmetic and copies ran while one was open for 4% of the time, Pallas kernels for 0%

commit v1 on v0

v1 whole, which is shorter than its diff:
```python
import functools
import math

import jax
import jax.numpy as jnp
from jax import lax
from jax.experimental import pallas as pl
from jax.experimental.pallas import tpu as pltpu
from jax.sharding import PartitionSpec as P

HEAD_DIM = 128
GROUP = 2
EPSILON = 1e-06
KV_PER_CHUNK = 2
F32 = jnp.float32
BF16 = jnp.bfloat16
MESH = pl.DeviceIdType.MESH


def each(low, high, body):
    if high - low <= 8:
        for i in range(low, high):
            body(i)
    else:
        lax.fori_loop(low, high, lambda i, x: (body(i), x)[1], 0)


def kernel(
    n, rows, scale, model_width,
    q_ref, k_hbm, v_hbm, w_hbm, gain_ref, out_ref,
    k_buf, v_buf, w_buf, q_all, part, arrived, lse_all, merged, proj, from_head, squares,
    k_sem, v_sem, w_sem, own_sem, q_send, q_fwd, q_recv, p_send, p_recv, l_send, l_recv,
    m_send, m_fwd, m_recv, h_send, h_recv, s_send, s_recv,
):
    chunks, tokens, chunk_width = q_all.shape
    kv_heads = k_buf.shape[0]
    chunk_heads = chunk_width // HEAD_DIM
    half = n // 2
    me = lax.axis_index("ctx")
    core = lax.axis_index("head")
    across = lax.rem(me, 2)
    along = me // 2
    partner = me + 1 - 2 * across

    def peer(k):
        return lax.rem(along + k, half) * 2 + across

    def other(k):
        return lax.rem(me + k, n)

    def block(i):
        return pl.ds(pl.multiple_of(i * rows, rows), rows)

    def lanes(j):
        return pl.ds(pl.multiple_of(j * HEAD_DIM, HEAD_DIM), HEAD_DIM)

    def k_copy(j):
        return pltpu.make_async_copy(k_hbm.at[:, lanes(j)], k_buf.at[j], k_sem.at[j])

    def v_copy(j):
        return pltpu.make_async_copy(v_hbm.at[:, lanes(j)], v_buf.at[j], v_sem.at[j])

    def w_copy(c):
        return pltpu.make_async_copy(
            w_hbm.at[pl.ds(pl.multiple_of(c * chunk_width, chunk_width), chunk_width), :],
            w_buf.at[c], w_sem.at[c])

    def own_copy(c):
        return pltpu.make_async_copy(
            q_ref.at[:, pl.ds(c * chunk_width, chunk_width)], q_all.at[c, block(me), :], own_sem.at[c])

    def q_copy(c, dest):
        return pltpu.make_async_remote_copy(
            src_ref=q_ref.at[:, pl.ds(c * chunk_width, chunk_width)],
            dst_ref=q_all.at[c, block(me), :],
            send_sem=q_send.at[c, dest], recv_sem=q_recv.at[c, me],
            device_id={"ctx": dest}, device_id_type=MESH)

    def gathered(ref, send, recv, c, source, dest):
        return pltpu.make_async_remote_copy(
            src_ref=ref.at[c, block(source), :], dst_ref=ref.at[c, block(source), :],
            send_sem=send.at[c, source], recv_sem=recv.at[c, source],
            device_id={"ctx": dest}, device_id_type=MESH)

    def m_copy(c, dest):
        return pltpu.make_async_remote_copy(
            src_ref=merged.at[c, block(me), :], dst_ref=merged.at[c, block(me), :],
            send_sem=m_send.at[c, dest], recv_sem=m_recv.at[c, me],
            device_id={"ctx": dest}, device_id_type=MESH)

    def p_copy(c, dest, source):
        return pltpu.make_async_remote_copy(
            src_ref=part.at[c, block(dest), :], dst_ref=arrived.at[c, source],
            send_sem=p_send.at[c, dest], recv_sem=p_recv.at[c, source],
            device_id={"ctx": dest}, device_id_type=MESH)

    def l_copy(c, dest, source):
        return pltpu.make_async_remote_copy(
            src_ref=lse_all.at[c, source], dst_ref=lse_all.at[c, source],
            send_sem=l_send.at[c, dest], recv_sem=l_recv.at[c, source],
            device_id={"ctx": dest}, device_id_type=MESH)

    def s_copy(dest, source):
        return pltpu.make_async_remote_copy(
            src_ref=squares.at[source], dst_ref=squares.at[source],
            send_sem=s_send.at[dest], recv_sem=s_recv.at[source],
            device_id={"ctx": dest}, device_id_type=MESH)

    barrier = pltpu.get_barrier_semaphore()
    each(1, n, lambda k: pl.semaphore_signal(
        barrier, inc=1, device_id={"ctx": other(k)}, device_id_type=MESH))
    pl.semaphore_signal(barrier, inc=1, device_id={"head": 1 - core}, device_id_type=MESH)
    for c in range(chunks):
        own_copy(c).start()
    for j in range(kv_heads):
        k_copy(j).start()
        v_copy(j).start()
    for c in range(chunks):
        w_copy(c).start()
    pl.semaphore_wait(barrier, n)

    def send_q(c):
        each(1, half, lambda k: q_copy(c, peer(k)).start())
        q_copy(c, partner).start()

    for c in range(chunks):
        send_q(c)

    def forward_q(c):
        def one(k):
            copy = gathered(q_all, q_fwd, q_recv, c, peer(half - k), partner)
            copy.wait_recv()
            copy.start()
        each(1, half, one)

    def wait_q(c):
        pltpu.make_async_copy(
            q_ref.at[:, pl.ds(0, chunk_width)], q_all.at[c, block(me), :], own_sem.at[c]).wait()
        def one(k):
            source = lax.rem(partner // 2 + k, half) * 2 + lax.rem(partner, 2)
            gathered(q_all, q_fwd, q_recv, c, source, partner).wait_recv()
        each(0, half, one)

    forward_q(0)
    proj[...] = jnp.zeros_like(proj)

    exponent = scale * math.log2(math.e)
    tile = min(tokens, 128)

    def attend(c):
        wait_q(c)
        for jj in range(KV_PER_CHUNK):
            j = c * KV_PER_CHUNK + jj
            k_copy(j).wait()
            v_copy(j).wait()
            def one(t, jj=jj, j=j):
                at = pl.ds(pl.multiple_of(t * tile, tile), tile)
                queries = jnp.concatenate(
                    [q_all[c, at, (jj * GROUP + g) * HEAD_DIM:(jj * GROUP + g + 1) * HEAD_DIM]
                     for g in range(GROUP)], axis=0)
                scores = lax.dot_general(
                    queries, k_buf[j], (((1,), (1,)), ((), ())), preferred_element_type=F32)
                maxima = jnp.max(scores, axis=1, keepdims=True)
                expo = jnp.exp2((scores - maxima) * exponent)
                totals = jnp.sum(expo, axis=1, keepdims=True)
                weighted = jnp.dot(expo.astype(BF16), v_buf[j], preferred_element_type=F32) / totals
                lse = maxima * scale + jnp.log(totals)
                weighted = weighted.astype(BF16)
                diagonal = (lax.broadcasted_iota(jnp.int32, (tile, tile), 0)
                            == lax.broadcasted_iota(jnp.int32, (tile, tile), 1))
                for g in range(GROUP):
                    r = jj * GROUP + g
                    part[c, at, r * HEAD_DIM:(r + 1) * HEAD_DIM] = weighted[g * tile:(g + 1) * tile]
                    row = jnp.sum(
                        jnp.where(diagonal, lse[g * tile:(g + 1) * tile], 0.0), axis=0, keepdims=True)
                    lse_all[c, me, r:r + 1, at] = row
            each(0, tokens // tile, one)
            if jj == 0:
                @pl.when(c + 1 < chunks)
                def _():
                    forward_q(c + 1)

        def send(k):
            dest = other(k)
            l_copy(c, dest, me).start()
            p_copy(c, dest, me).start()
        each(1, n, send)

    def merge(c):
        def arrive(k):
            source = other(k)
            l_copy(c, me, source).wait_recv()
            p_copy(c, me, source).wait_recv()
        each(1, n, arrive)
        lse = lse_all[c]
        peak = jnp.max(lse, axis=0)
        whole = peak + jnp.log(jnp.sum(jnp.exp(lse - peak[None]), axis=0))
        mine = (lax.broadcasted_iota(jnp.int32, (rows, tokens), 1)
                == me * rows + lax.broadcasted_iota(jnp.int32, (rows, tokens), 0))
        total = [None] * chunk_heads
        for k in range(n):
            source = other(k)
            weight = jnp.exp(lse_all[c, source] - whole)
            values = part[c, block(me), :] if k == 0 else arrived[c, source]
            for h in range(chunk_heads):
                column = jnp.sum(jnp.where(mine, weight[h:h + 1], 0.0), axis=1, keepdims=True)
                term = values[:, h * HEAD_DIM:(h + 1) * HEAD_DIM].astype(F32) * column
                total[h] = term if k == 0 else total[h] + term
        for h in range(chunk_heads):
            merged[c, block(me), h * HEAD_DIM:(h + 1) * HEAD_DIM] = total[h].astype(BF16)
        each(1, half, lambda k: m_copy(c, peer(k)).start())
        m_copy(c, partner).start()

    def forward_m(c):
        def one(k):
            copy = gathered(merged, m_fwd, m_recv, c, peer(half - k), partner)
            copy.wait_recv()
            copy.start()
        each(1, half, one)

    def project(c):
        def one(k):
            source = lax.rem(partner // 2 + k, half) * 2 + lax.rem(partner, 2)
            gathered(merged, m_fwd, m_recv, c, source, partner).wait_recv()
        each(0, half, one)
        w_copy(c).wait()
        proj[...] += jnp.dot(merged[c], w_buf[c], preferred_element_type=F32)

    def step(t, carry):
        @pl.when(t < chunks)
        def _():
            attend(t)

        @pl.when((t >= 1) & (t <= chunks))
        def _():
            merge(t - 1)

        @pl.when((t >= 2) & (t <= chunks + 1))
        def _():
            forward_m(t - 2)

        @pl.when(t >= 3)
        def _():
            project(t - 3)
        return carry

    lax.fori_loop(0, chunks + 3, step, 0)

    split = tokens // 2
    def rows_of(i):
        return pl.ds(pl.multiple_of(i * split, split), split)
    exchange = pltpu.make_async_remote_copy(
        src_ref=proj.at[rows_of(1 - core), :], dst_ref=from_head, send_sem=h_send, recv_sem=h_recv,
        device_id={"head": 1 - core}, device_id_type=MESH)
    exchange.start()
    exchange.wait()
    summed = proj[rows_of(core), :] + from_head[...]
    square = jnp.sum(summed * summed, axis=1, keepdims=True)
    diagonal = (lax.broadcasted_iota(jnp.int32, (split, split), 0)
                == lax.broadcasted_iota(jnp.int32, (split, split), 1))
    squares[me] = jnp.broadcast_to(
        jnp.sum(jnp.where(diagonal, square, 0.0), axis=0, keepdims=True), (8, split))
    each(1, n, lambda k: s_copy(other(k), me).start())
    each(1, n, lambda k: s_copy(me, other(k)).wait_recv())
    square_row = jnp.sum(squares[...], axis=0)[0:1]
    square_sums = jnp.sum(jnp.where(diagonal, square_row, 0.0), axis=1, keepdims=True)
    normed = summed * lax.rsqrt(square_sums / model_width + EPSILON) * gain_ref[...]
    out_ref[...] = normed.astype(BF16)

    def drain(c, carry):
        def sent_gather(k):
            gathered(q_all, q_send, q_recv, c, peer(k), partner).wait_send()
            gathered(q_all, q_fwd, q_recv, c, peer(k), partner).wait_send()
            m_copy(c, peer(k)).wait_send()
            gathered(merged, m_fwd, m_recv, c, peer(k), partner).wait_send()
        each(1, half, sent_gather)
        gathered(q_all, q_send, q_recv, c, partner, partner).wait_send()
        m_copy(c, partner).wait_send()
        def sent_part(k):
            l_copy(c, other(k), me).wait_send()
            p_copy(c, other(k), me).wait_send()
        each(1, n, sent_part)
        return carry
    lax.fori_loop(0, chunks, drain, 0)
    each(1, n, lambda k: s_copy(other(k), me).wait_send())


def local(model_heads, queries, cache_keys, cache_values, out_weight, norm_gain):
    n = lax.axis_size("ctx")
    rows, width = queries.shape
    keys, kv_width = cache_keys.shape
    kv_heads = kv_width // HEAD_DIM
    columns = out_weight.shape[1]
    tokens = rows * n
    model_width = columns * n
    chunks = kv_heads // KV_PER_CHUNK
    chunk_width = width // chunks
    scale = float(model_width // model_heads) ** (-0.5)
    dma = pltpu.SemaphoreType.DMA
    any_space = pl.BlockSpec(memory_space=pl.ANY)
    vmem = pl.BlockSpec(memory_space=pltpu.VMEM)
    return pl.pallas_call(
        functools.partial(kernel, n, rows, scale, model_width),
        out_shape=jax.ShapeDtypeStruct((tokens // 2, columns), BF16),
        in_specs=[vmem, any_space, any_space, any_space, vmem],
        out_specs=vmem,
        scratch_shapes=[
            pltpu.VMEM((kv_heads, keys, HEAD_DIM), BF16),
            pltpu.VMEM((kv_heads, keys, HEAD_DIM), BF16),
            pltpu.VMEM((chunks, chunk_width, columns), BF16),
            pltpu.VMEM((chunks, tokens, chunk_width), BF16),
            pltpu.VMEM((chunks, tokens, chunk_width), BF16),
            pltpu.VMEM((chunks, n, rows, chunk_width), BF16),
            pltpu.VMEM((chunks, n, chunk_width // HEAD_DIM, tokens), F32),
            pltpu.VMEM((chunks, tokens, chunk_width), BF16),
            pltpu.VMEM((tokens, columns), F32),
            pltpu.VMEM((tokens // 2, columns), F32),
            pltpu.VMEM((n, 8, tokens // 2), F32),
            dma((kv_heads,)), dma((kv_heads,)), dma((chunks,)), dma((chunks,)),
            dma((chunks, n)), dma((chunks, n)), dma((chunks, n)),
            dma((chunks, n)), dma((chunks, n)), dma((chunks, n)), dma((chunks, n)),
            dma((chunks, n)), dma((chunks, n)), dma((chunks, n)),
            dma, dma, dma((n,)), dma((n,)),
        ],
        compiler_params=pltpu.CompilerParams(
            collective_id=0, has_side_effects=True, vmem_limit_bytes=56 * 1024 * 1024),
    )(queries, cache_keys, cache_values, out_weight, norm_gain[None, :])


def solution(mesh):
    in_specs = (
        P(("groups", "ctx"), "head"),
        P(("groups", "ctx"), "head"),
        P(("groups", "ctx"), "head"),
        P("head", "ctx"),
        P("ctx"),
    )
    out_specs = P(("groups", "head"), "ctx")

    def whole(queries, *rest):
        body = functools.partial(local, queries.shape[1] // HEAD_DIM)
        return jax.shard_map(
            body, mesh=mesh, in_specs=in_specs, out_specs=out_specs, check_vma=False)(queries, *rest)
    return whole
```

time: 192 us -> 58.4 us (0.30)
  blocking collectives: 86.2 us -> 0 us
  Pallas kernels: 0 us -> 50.7 us
  matrix products: 26.5 us -> 0 us
  waiting for transfers between devices: 16.9 us -> 0 us
  between operations: 13.5 us -> 0.01 us
  local copies, waits for them, and re-layouts: 19.1 us -> 7.38 us
  loops' own time: 11.5 us -> 0 us
  starting transfers between devices: 9.23 us -> 0 us
  other arithmetic: 7.27 us -> 0 us
    all_gather x2 -> x0, blocking collectives: 64.6 us -> none  [the longest x1 33.3 us: local(): all_queries = lax.all_gather(queries, 'ctx', axis=0, tiled=True)]
    pallas_call x0 -> x1, Pallas kernels: none -> 50.7 us  [local(): pl.pallas_call(functools.partial(kernel, n, rows, scale, model_width), ou...]
    dot_general x17 -> x0, matrix products: 26.5 us -> none  [the longest x8 12.5 us: one_head(): jnp.einsum('grk,kd->rgd', probabilities, value_part, preferred_element_ty...]
    psum x1 -> x0, blocking collectives: 21.6 us -> none  [local(): square_sums = lax.psum(jnp.sum(summed * summed, axis=1), 'ctx')]
    another operation x1 -> x0, loops' own time: 11.5 us -> none  [attend(): lax.map(one_head, jnp.arange(pair_count, dtype=jnp.int32))]
    all_to_all x2 -> x0, waiting for transfers between devices: 9.76 us -> none  [the longest x1 5.63 us: local(): lax.all_to_all(grouped_out.astype(jnp.float32), 'ctx', split_axis=0, conc...]
    all_to_all x2 -> x0, starting transfers between devices: 9.19 us -> none  [the longest x1 5.7 us: local(): lax.all_to_all(grouped_lse, 'ctx', split_axis=0, concat_axis=0, tiled=True)]
    reduce_scatter x1 -> x0, waiting for transfers between devices: 7.12 us -> none  [local(): lax.psum_scatter(projected, 'head', scatter_dimension=0, tiled=True)]
  transfers between devices with their start and end apart: 3 -> 0, of which waited for: 3 -> 0; matrix products, arithmetic and copies ran while one was open for 4% -> 0% of each run, Pallas kernels for 0% -> 0%
where the time goes in v1:
time: 58.4 us; the launch traced here: 58.1 us
  Pallas kernels  50.7 us (87%)
  local copies, waits for them, and re-layouts  7.38 us (13%)
    pallas_call x1, Pallas kernels, local(): pl.pallas_call(functools.partial(kernel, n, rows, scale, model_width), ou...  50.7 us
    unnamed x2, local copies, waits for them, and re-layouts  6.11 us
    broadcast_in_dim x1, local copies, waits for them, and re-layouts, local(): norm_gain[None, :]  1.27 us

profile of v1, /device:TPU:0, one launch (start us, length us, event | category | flops | bytes accessed | tf_op | source)
XLA Modules:
  0.0 58.1 jit_solution(1253818641648428963)
XLA Ops:
  0.0 1.3 %broadcast_in_dim.3.gain_ref = f32[1,672]{1,0:T(1,128)} reshape(f32[672]{0:T(1024)} %param.9) | data formatting | bytes 5376 | tf_op jit(solution)/shard_map/broadcast_in_dim | solution.py:327
  1.3 4.6 %copy.6.w_hbm = bf16[2048,672]{1,0:T(8,128)(2,1)} copy(bf16[2048,672]{0,1:T(8,128)(2,1)} %param.8) | data formatting | bytes 5505024 | tf_op args[3]
  5.8 50.7 %shard_map.55 = bf16[64,672]{1,0:T(8,128)(2,1)} custom-call(bf16[16,2048]{1,0:T(8,128)(2,1)} %q_ref.1, bf16[2048,1024]{1,0:T(8,128)(2,1)} %k_hbm.1, bf16[2048,1024]{1,0:T(8,128)(2,1)} %v_hbm.1, bf16[2048,672]{1,0:T(8,128)(2,1)} %copy.6.w_hbm, f32[1,672]{1,0:T(1,128)} %broadcast_in_dim.3.gain_ref), custom_call_target="tpu_custom_call" | custom-call | tf_op jit(solution)/shard_map/pallas_call | solution.py:302
  56.6 1.5 %copy.8 = bf16[64,672]{1,0:T(8,128)(2,1)} copy(bf16[64,672]{1,0:T(8,128)(2,1)} %shard_map.55) | data formatting | bytes 172032

commit v2 on v1

--- a/solution.py
+++ b/solution.py
@@ -11,7 +11,7 @@
 HEAD_DIM = 128
 GROUP = 2
 EPSILON = 1e-06
-KV_PER_CHUNK = 2
+KV_PER_CHUNK = 4
 F32 = jnp.float32
 BF16 = jnp.bfloat16
 MESH = pl.DeviceIdType.MESH
@@ -27,7 +27,7 @@
 
 def kernel(
     n, rows, scale, model_width,
-    q_ref, k_hbm, v_hbm, w_hbm, gain_ref, out_ref,
+    q_ref, k_hbm, v_hbm, w_hbm, out_ref,
     k_buf, v_buf, w_buf, q_all, part, arrived, lse_all, merged, proj, from_head, squares,
     k_sem, v_sem, w_sem, own_sem, q_send, q_fwd, q_recv, p_send, p_recv, l_send, l_recv,
     m_send, m_fwd, m_recv, h_send, h_recv, s_send, s_recv,
@@ -62,7 +62,7 @@
 
     def w_copy(c):
         return pltpu.make_async_copy(
-            w_hbm.at[pl.ds(pl.multiple_of(c * chunk_width, chunk_width), chunk_width), :],
+            w_hbm.at[:, pl.ds(pl.multiple_of(c * chunk_width, chunk_width), chunk_width)],
             w_buf.at[c], w_sem.at[c])
 
     def own_copy(c):
@@ -224,7 +224,8 @@
             gathered(merged, m_fwd, m_recv, c, source, partner).wait_recv()
         each(0, half, one)
         w_copy(c).wait()
-        proj[...] += jnp.dot(merged[c], w_buf[c], preferred_element_type=F32)
+        proj[...] += lax.dot_general(
+            merged[c], w_buf[c], (((1,), (1,)), ((), ())), preferred_element_type=F32)
 
     def step(t, carry):
         @pl.when(t < chunks)
@@ -264,8 +265,7 @@
     each(1, n, lambda k: s_copy(me, other(k)).wait_recv())
     square_row = jnp.sum(squares[...], axis=0)[0:1]
     square_sums = jnp.sum(jnp.where(diagonal, square_row, 0.0), axis=1, keepdims=True)
-    normed = summed * lax.rsqrt(square_sums / model_width + EPSILON) * gain_ref[...]
-    out_ref[...] = normed.astype(BF16)
+    out_ref[...] = summed * lax.rsqrt(square_sums / model_width + EPSILON)
 
     def drain(c, carry):
         def sent_gather(k):
@@ -299,15 +299,15 @@
     dma = pltpu.SemaphoreType.DMA
     any_space = pl.BlockSpec(memory_space=pl.ANY)
     vmem = pl.BlockSpec(memory_space=pltpu.VMEM)
-    return pl.pallas_call(
+    normed = pl.pallas_call(
         functools.partial(kernel, n, rows, scale, model_width),
-        out_shape=jax.ShapeDtypeStruct((tokens // 2, columns), BF16),
-        in_specs=[vmem, any_space, any_space, any_space, vmem],
+        out_shape=jax.ShapeDtypeStruct((tokens // 2, columns), F32),
+        in_specs=[vmem, any_space, any_space, any_space],
         out_specs=vmem,
         scratch_shapes=[
             pltpu.VMEM((kv_heads, keys, HEAD_DIM), BF16),
             pltpu.VMEM((kv_heads, keys, HEAD_DIM), BF16),
-            pltpu.VMEM((chunks, chunk_width, columns), BF16),
+            pltpu.VMEM((chunks, columns, chunk_width), BF16),
             pltpu.VMEM((chunks, tokens, chunk_width), BF16),
             pltpu.VMEM((chunks, tokens, chunk_width), BF16),
             pltpu.VMEM((chunks, n, rows, chunk_width), BF16),
@@ -324,7 +324,8 @@
         ],
         compiler_params=pltpu.CompilerParams(
             collective_id=0, has_side_effects=True, vmem_limit_bytes=56 * 1024 * 1024),
-    )(queries, cache_keys, cache_values, out_weight, norm_gain[None, :])
+    )(queries, cache_keys, cache_values, out_weight.T)
+    return (normed * norm_gain[None, :]).astype(BF16)
 
 
 def solution(mesh):

time: 58.4 us -> 51 us (0.87)
  local copies, waits for them, and re-layouts: 7.38 us -> 0.01 us
  other arithmetic: 0 us -> 1.58 us
  Pallas kernels: 50.7 us -> 49.2 us
    unnamed x2, local copies, waits for them, and re-layouts: 6.11 us -> 0.01 us
    convert_element_type x0 -> x1, other arithmetic: none -> 1.58 us  [local(): return (normed * norm_gain[None, :]).astype(BF16)]
    pallas_call x1, Pallas kernels: 50.7 us -> 49.2 us  [local(): pl.pallas_call(functools.partial(kernel, n, rows, scale, model_width), ou...]
    broadcast_in_dim x1 -> x0, local copies, waits for them, and re-layouts: 1.27 us -> none  [local(): norm_gain[None, :]]
where the time goes in v2:
time: 51 us; the launch traced here: 50.8 us
  Pallas kernels  49.2 us (96%)
  other arithmetic  1.58 us (3%)
    pallas_call x1, Pallas kernels, local(): pl.pallas_call(functools.partial(kernel, n, rows, scale, model_width), ou...  49.2 us
    convert_element_type x1, other arithmetic, local(): return (normed * norm_gain[None, :]).astype(BF16)  1.58 us

profile of v2, /device:TPU:0, one launch (start us, length us, event | category | flops | bytes accessed | tf_op | source)
XLA Modules:
  0.0 50.8 jit_solution(15597292274803699260)
XLA Ops:
  0.0 0.0 copy-start
  0.0 49.2 %shard_map.55 = f32[64,672]{1,0:T(8,128)} custom-call(bf16[16,2048]{1,0:T(8,128)(2,1)} %q_ref.1, bf16[2048,1024]{1,0:T(8,128)(2,1)} %k_hbm.1, bf16[2048,1024]{1,0:T(8,128)(2,1)} %v_hbm.1, bf16[672,2048]{1,0:T(8,128)(2,1)} %bitcast.1), custom_call_target="tpu_custom_call" | custom-call | tf_op jit(solution)/shard_map/pallas_call | solution.py:302
  49.2 0.0 copy-done
  49.2 1.6 %multiply_convert_fusion = bf16[64,672]{1,0:T(8,128)(2,1)} fusion(f32[64,672]{1,0:T(8,128)} %shard_map.55, f32[672]{0:T(1024)S(1)} %copy-done), kind=kLoop, calls=%fused_computation | loop fusion | flops 86016 | bytes 260736 | tf_op jit(solution)/shard_map/convert_element_type | solution.py:328
Async XLA Ops:
  0.0 49.2 %copy-start = (f32[672]{0:T(1024)S(1)}, f32[672]{0:T(1024)}, u32[]{:S(2)}) copy-start(f32[672]{0:T(1024)} %param.9) | copy-start | bytes 8068

commit v3 on v2

--- a/solution.py
+++ b/solution.py
@@ -12,6 +12,7 @@
 GROUP = 2
 EPSILON = 1e-06
 KV_PER_CHUNK = 4
+KV_PER_SEND = 2
 F32 = jnp.float32
 BF16 = jnp.bfloat16
 MESH = pl.DeviceIdType.MESH
@@ -32,7 +33,8 @@
     k_sem, v_sem, w_sem, own_sem, q_send, q_fwd, q_recv, p_send, p_recv, l_send, l_recv,
     m_send, m_fwd, m_recv, h_send, h_recv, s_send, s_recv,
 ):
-    chunks, tokens, chunk_width = q_all.shape
+    q_chunks, tokens, q_width = q_all.shape
+    chunks, _, chunk_width = part.shape
     kv_heads = k_buf.shape[0]
     chunk_heads = chunk_width // HEAD_DIM
     half = n // 2
@@ -67,11 +69,11 @@
 
     def own_copy(c):
         return pltpu.make_async_copy(
-            q_ref.at[:, pl.ds(c * chunk_width, chunk_width)], q_all.at[c, block(me), :], own_sem.at[c])
+            q_ref.at[:, pl.ds(c * q_width, q_width)], q_all.at[c, block(me), :], own_sem.at[c])
 
     def q_copy(c, dest):
         return pltpu.make_async_remote_copy(
-            src_ref=q_ref.at[:, pl.ds(c * chunk_width, chunk_width)],
+            src_ref=q_ref.at[:, pl.ds(c * q_width, q_width)],
             dst_ref=q_all.at[c, block(me), :],
             send_sem=q_send.at[c, dest], recv_sem=q_recv.at[c, me],
             device_id={"ctx": dest}, device_id_type=MESH)
@@ -110,7 +112,7 @@
     each(1, n, lambda k: pl.semaphore_signal(
         barrier, inc=1, device_id={"ctx": other(k)}, device_id_type=MESH))
     pl.semaphore_signal(barrier, inc=1, device_id={"head": 1 - core}, device_id_type=MESH)
-    for c in range(chunks):
+    for c in range(q_chunks):
         own_copy(c).start()
     for j in range(kv_heads):
         k_copy(j).start()
@@ -123,7 +125,7 @@
         each(1, half, lambda k: q_copy(c, peer(k)).start())
         q_copy(c, partner).start()
 
-    for c in range(chunks):
+    for c in range(q_chunks):
         send_q(c)
 
     def forward_q(c):
@@ -135,28 +137,31 @@
 
     def wait_q(c):
         pltpu.make_async_copy(
-            q_ref.at[:, pl.ds(0, chunk_width)], q_all.at[c, block(me), :], own_sem.at[c]).wait()
+            q_ref.at[:, pl.ds(0, q_width)], q_all.at[c, block(me), :], own_sem.at[c]).wait()
         def one(k):
             source = lax.rem(partner // 2 + k, half) * 2 + lax.rem(partner, 2)
             gathered(q_all, q_fwd, q_recv, c, source, partner).wait_recv()
         each(0, half, one)
 
-    forward_q(0)
+    for c in range(min(2, q_chunks)):
+        forward_q(c)
     proj[...] = jnp.zeros_like(proj)
 
     exponent = scale * math.log2(math.e)
     tile = min(tokens, 128)
 
     def attend(c):
-        wait_q(c)
         for jj in range(KV_PER_CHUNK):
+            sent = c * (KV_PER_CHUNK // KV_PER_SEND) + jj // KV_PER_SEND
+            if jj % KV_PER_SEND == 0:
+                wait_q(sent)
             j = c * KV_PER_CHUNK + jj
             k_copy(j).wait()
             v_copy(j).wait()
-            def one(t, jj=jj, j=j):
+            def one(t, jj=jj, j=j, sent=sent, lane=jj % KV_PER_SEND * GROUP):
                 at = pl.ds(pl.multiple_of(t * tile, tile), tile)
                 queries = jnp.concatenate(
-                    [q_all[c, at, (jj * GROUP + g) * HEAD_DIM:(jj * GROUP + g + 1) * HEAD_DIM]
+                    [q_all[sent, at, (lane + g) * HEAD_DIM:(lane + g + 1) * HEAD_DIM]
                      for g in range(GROUP)], axis=0)
                 scores = lax.dot_general(
                     queries, k_buf[j], (((1,), (1,)), ((), ())), preferred_element_type=F32)
@@ -175,10 +180,10 @@
                         jnp.where(diagonal, lse[g * tile:(g + 1) * tile], 0.0), axis=0, keepdims=True)
                     lse_all[c, me, r:r + 1, at] = row
             each(0, tokens // tile, one)
-            if jj == 0:
-                @pl.when(c + 1 < chunks)
-                def _():
-                    forward_q(c + 1)
+            if jj % KV_PER_SEND == 0:
+                @pl.when(sent + 2 < q_chunks)
+                def _(sent=sent):
+                    forward_q(sent + 2)
 
         def send(k):
             dest = other(k)
@@ -262,19 +267,18 @@
     squares[me] = jnp.broadcast_to(
         jnp.sum(jnp.where(diagonal, square, 0.0), axis=0, keepdims=True), (8, split))
     each(1, n, lambda k: s_copy(other(k), me).start())
-    each(1, n, lambda k: s_copy(me, other(k)).wait_recv())
-    square_row = jnp.sum(squares[...], axis=0)[0:1]
-    square_sums = jnp.sum(jnp.where(diagonal, square_row, 0.0), axis=1, keepdims=True)
-    out_ref[...] = summed * lax.rsqrt(square_sums / model_width + EPSILON)
+    def drain_q(c, carry):
+        each(1, half, lambda k: gathered(q_all, q_send, q_recv, c, peer(k), partner).wait_send())
+        each(1, half, lambda k: gathered(q_all, q_fwd, q_recv, c, peer(k), partner).wait_send())
+        gathered(q_all, q_send, q_recv, c, partner, partner).wait_send()
+        return carry
+    lax.fori_loop(0, q_chunks, drain_q, 0)
 
     def drain(c, carry):
         def sent_gather(k):
-            gathered(q_all, q_send, q_recv, c, peer(k), partner).wait_send()
-            gathered(q_all, q_fwd, q_recv, c, peer(k), partner).wait_send()
             m_copy(c, peer(k)).wait_send()
             gathered(merged, m_fwd, m_recv, c, peer(k), partner).wait_send()
         each(1, half, sent_gather)
-        gathered(q_all, q_send, q_recv, c, partner, partner).wait_send()
         m_copy(c, partner).wait_send()
         def sent_part(k):
             l_copy(c, other(k), me).wait_send()
@@ -282,6 +286,11 @@
         each(1, n, sent_part)
         return carry
     lax.fori_loop(0, chunks, drain, 0)
+    each(1, n, lambda k: s_copy(me, other(k)).wait_recv())
+    square_row = jnp.sum(squares[...], axis=0)[0:1]
+    square_sums = jnp.sum(jnp.where(diagonal, square_row, 0.0), axis=1, keepdims=True)
+    out_ref[...] = summed * lax.rsqrt(square_sums / model_width + EPSILON)
+
     each(1, n, lambda k: s_copy(other(k), me).wait_send())
 
 
@@ -295,6 +304,7 @@
     model_width = columns * n
     chunks = kv_heads // KV_PER_CHUNK
     chunk_width = width // chunks
+    q_chunks = kv_heads // KV_PER_SEND
     scale = float(model_width // model_heads) ** (-0.5)
     dma = pltpu.SemaphoreType.DMA
     any_space = pl.BlockSpec(memory_space=pl.ANY)
@@ -308,7 +318,7 @@
             pltpu.VMEM((kv_heads, keys, HEAD_DIM), BF16),
             pltpu.VMEM((kv_heads, keys, HEAD_DIM), BF16),
             pltpu.VMEM((chunks, columns, chunk_width), BF16),
-            pltpu.VMEM((chunks, tokens, chunk_width), BF16),
+            pltpu.VMEM((q_chunks, tokens, width // q_chunks), BF16),
             pltpu.VMEM((chunks, tokens, chunk_width), BF16),
             pltpu.VMEM((chunks, n, rows, chunk_width), BF16),
             pltpu.VMEM((chunks, n, chunk_width // HEAD_DIM, tokens), F32),
@@ -316,8 +326,8 @@
             pltpu.VMEM((tokens, columns), F32),
             pltpu.VMEM((tokens // 2, columns), F32),
             pltpu.VMEM((n, 8, tokens // 2), F32),
-            dma((kv_heads,)), dma((kv_heads,)), dma((chunks,)), dma((chunks,)),
-            dma((chunks, n)), dma((chunks, n)), dma((chunks, n)),
+            dma((kv_heads,)), dma((kv_heads,)), dma((chunks,)), dma((q_chunks,)),
+            dma((q_chunks, n)), dma((q_chunks, n)), dma((q_chunks, n)),
             dma((chunks, n)), dma((chunks, n)), dma((chunks, n)), dma((chunks, n)),
             dma((chunks, n)), dma((chunks, n)), dma((chunks, n)),
             dma, dma, dma((n,)), dma((n,)),

time: 51 us -> 50.1 us (0.982)
  Pallas kernels: 49.2 us -> 48.3 us
    pallas_call x1, Pallas kernels: 49.2 us -> 48.3 us  [local(): pl.pallas_call(functools.partial(kernel, n, rows, scale, model_width), ou...]
where the time goes in v3:
time: 50.1 us; the launch traced here: 49.9 us
  Pallas kernels  48.3 us (96%)
  other arithmetic  1.58 us (3%)
    pallas_call x1, Pallas kernels, local(): pl.pallas_call(functools.partial(kernel, n, rows, scale, model_width), ou...  48.3 us
    convert_element_type x1, other arithmetic, local(): return (normed * norm_gain[None, :]).astype(BF16)  1.58 us

profile of v3, /device:TPU:0, one launch (start us, length us, event | category | flops | bytes accessed | tf_op | source)
XLA Modules:
  0.0 49.9 jit_solution(16557713264246439462)
XLA Ops:
  0.0 0.0 copy-start
  0.0 48.3 %shard_map.55 = f32[64,672]{1,0:T(8,128)} custom-call(bf16[16,2048]{1,0:T(8,128)(2,1)} %q_ref.1, bf16[2048,1024]{1,0:T(8,128)(2,1)} %k_hbm.1, bf16[2048,1024]{1,0:T(8,128)(2,1)} %v_hbm.1, bf16[672,2048]{1,0:T(8,128)(2,1)} %bitcast.1), custom_call_target="tpu_custom_call" | custom-call | tf_op jit(solution)/shard_map/pallas_call | solution.py:312
  48.3 0.0 copy-done
  48.3 1.6 %multiply_convert_fusion = bf16[64,672]{1,0:T(8,128)(2,1)} fusion(f32[64,672]{1,0:T(8,128)} %shard_map.55, f32[672]{0:T(1024)S(1)} %copy-done), kind=kLoop, calls=%fused_computation | loop fusion | flops 86016 | bytes 260736 | tf_op jit(solution)/shard_map/convert_element_type | solution.py:338
Async XLA Ops:
  0.0 48.3 %copy-start = (f32[672]{0:T(1024)S(1)}, f32[672]{0:T(1024)}, u32[]{:S(2)}) copy-start(f32[672]{0:T(1024)} %param.9) | copy-start | bytes 8068
